TPU v7x, 256 devices: a whole 4x4x8 slice. The times are simulated.
256 devices in a mesh: dp: 16 (over z_hi, y), row: 2 (over z_lo), col: 8 (over x, core).
Axes of the slice: x: 4, y: 4, z: 8 (z_hi: 4, z_lo: 2; z = z_hi * 2 + z_lo), core: 2. Of those that a mesh axis runs over, the one named last changes fastest.
Arguments:
- activations: bfloat16 [16384, 4096], P('dp', 'row'), may hold values from -160 to 160, as said below
- cotangent: bfloat16 [16384, 16384], P('dp', 'col'), may hold values from -0.03125 to 0.03125, as said below
- row_old: float32 [4096], P(('row', 'dp')), may hold values from 1 to 70, as said below
- col_old: float32 [16384], P('col'), may hold values from 0.02 to 0.3
Outputs:
- update: float32 [4096, 16384], P(('row', 'dp'), 'col')
- row_new: float32 [4096], P(('row', 'dp'))
- col_new: float32 [16384], P('col')
- update_rms: float32 [], replicated
Inputs may be any that keep to these rules, and one draw needn't show every extreme that they name: activations of feature columns of differing scales. cotangent columns of differing scales. `row_old`: positive entries of differing scales.
All inputs are finite; a program needn't handle non-finite values.
Results may differ from a plain program's by a relative error of at most 0.0003.
Values sent between devices are 32-bit elements; how exact they have to be, the bound alone decides.
No kernel may reach another device: no remote copies, remote signals or barrier semaphores. Data moves between devices by JAX's collectives and lax.ppermute only.
A program may use at most 128 MiB of HBM per device.

v0:
```python
import jax
import jax.numpy as jnp
from jax import lax
from jax.experimental import pallas as pl
from jax.experimental.pallas import tpu as pltpu
from jax.sharding import Mesh, PartitionSpec as P

D = 4096
FF = 16384


DECAY = 0.5
EPS_ONE = 1e-30
CLIP = 0.25

AXES = ("zh", "y", "zl", "x", "c")
COLS = {
    "a": (0, 256), "b": (256, 768), "c": (768, 1280),
    "d": (1280, 1536), "f": (1536, 1664), "e": (1664, 2048),
}


def swap(value, axis, step):
    pairs = []
    for i in range(4):
        for core in range(2):
            other = i ^ 1 if core == step else i ^ 3
            pairs.append((2 * i + core, 2 * other + core))
    return lax.ppermute(value, (axis, "c"), pairs)


def spread_sum(value, axes, count):
    copies = jnp.broadcast_to(value[None], (count,) + value.shape)
    return jnp.sum(lax.all_to_all(copies, axes, 0, 0), axis=0)


def after(value, other):
    return lax.optimization_barrier((value, other))[0]


def first_kernel(blocks, rows, cols, out):
    out[...] = lax.dot_general(
        rows[...], cols[...], (((0,), (0,)), ((), ())), preferred_element_type=jnp.float32)


def second_kernel(blocks, rows, cols, out, by_y, by_zh):
    part = rows[...].T
    by_y[...] = part
    by_zh[...] = part

    @pl.when(pl.program_id(0) < 8)
    def _():
        out[...] = jnp.dot(part, cols[...], preferred_element_type=jnp.float32)


def early_product(kernel, blocks, rows, cols):
    depth, width = cols.shape
    count = blocks.shape[0]
    out_specs = [pl.BlockSpec((128, width), lambda i, blocks: (jnp.minimum(i, 7), 0))]
    out_shape = [jax.ShapeDtypeStruct((1024, width), jnp.float32)]
    if count == 16:
        out_specs += [
            pl.BlockSpec((128, depth), lambda i, blocks: (i, 0)),
            pl.BlockSpec((128, depth), lambda i, blocks: (4 * (i % 4) + i // 4, 0)),
        ]
        out_shape += [jax.ShapeDtypeStruct((2048, depth), rows.dtype)] * 2
    return pl.pallas_call(
        kernel,
        grid_spec=pltpu.PrefetchScalarGridSpec(
            num_scalar_prefetch=1,
            grid=(count,),
            in_specs=[
                pl.BlockSpec((depth, 128), lambda i, blocks: (0, blocks[i])),
                pl.BlockSpec((depth, width), lambda i, blocks: (0, 0)),
            ],
            out_specs=out_specs,
        ),
        out_shape=out_shape,
        compiler_params=pltpu.CompilerParams(vmem_limit_bytes=8 * 2**20),
        cost_estimate=pl.CostEstimate(
            flops=2 * 1024 * depth * width, bytes_accessed=8 * 2**20, transcendentals=0),
    )(blocks, rows, cols)


class Order:
    def __init__(self):
        self.last = None

    def __call__(self, value):
        if self.last is not None:
            value = after(value, self.last)
        self.last = value
        return value


class Chain:
    def __init__(self, order, axis, part):
        self.order, self.axis, self.part = order, axis, part

    def start(self):
        self.moved = swap(self.order(self.part(0)), self.axis, 0)

    def turn(self):
        got = self.order(self.moved)
        half = got.shape[0] // 2
        self.kept = got[:half]
        self.moved = swap(self.order(got[half:] + self.part(1)), self.axis, 1)

    def done(self):
        self.value = (self.order(self.moved) + self.kept) + self.part(2)


def summed_product(activations, cotangent):
    core = lax.axis_index("c")
    order = Order()

    def owners(axis):
        mine = lax.axis_index(axis)
        near, far = mine ^ 1, mine ^ 3
        return jnp.stack([
            jnp.where(core == 0, near, far), mine ^ 2, jnp.where(core == 0, far, near), mine,
        ]).astype(jnp.int32)

    def columns(chunk):
        return cotangent[:, slice(*COLS[chunk])]

    def quarters(rows):
        size = rows.shape[0] // 4
        return (rows[:2 * size], rows[2 * size:3 * size], rows[3 * size:])

    def product_chain(axis, chunk, first=None):
        def part(i):
            if i == 0 and first is not None:
                return first
            return jnp.dot(lhs[axis][i], columns(chunk), preferred_element_type=jnp.float32)

        return Chain(order, axis, part)

    def next_chain(chain):
        parts = quarters(chain.value)
        return Chain(order, "zh" if chain.axis == "y" else "y", lambda i: parts[i])

    blocks = (owners("y")[:, None] + 4 * owners("zh")[None, :]).reshape(16)
    first, = early_product(first_kernel, blocks[:8], activations, columns("a"))
    a = product_chain("y", "a", first)
    a.start()
    first, by_y, by_zh = early_product(second_kernel, blocks, order(activations), columns("b"))
    lhs = {"y": quarters(by_y), "zh": quarters(by_zh)}
    b = product_chain("y", "b", first)
    b.start()
    c, d, f = (product_chain("y", chunk) for chunk in "cdf")
    e = product_chain("zh", "e")
    e.start()
    a.turn()
    a.done()
    c.start()
    a = next_chain(a)
    a.start()
    b.turn()
    e.turn()
    a.turn()
    b.done()
    c.turn()
    b = next_chain(b)
    b.start()
    a.done()
    e.done()
    e = next_chain(e)
    e.start()
    d.start()
    b.turn()
    c.done()
    c = next_chain(c)
    c.start()
    f.start()
    d.turn()
    e.turn()
    f.turn()
    b.done()
    c.turn()
    d.done()
    d = next_chain(d)
    d.start()
    f.done()
    f = next_chain(f)
    f.start()
    d.turn()
    f.turn()
    e.done()
    c.done()
    d.done()
    f.done()
    return [chain.value for chain in (a, b, c, d, f, e)]


def per_device(activations, cotangent, row_old, col_old):
    grads = summed_product(activations, cotangent)
    squares = [g * g + EPS_ONE for g in grads]
    col_total = jnp.concatenate([jnp.sum(s, axis=0) for s in squares])
    row_total = sum(jnp.sum(s, axis=1) for s in squares)
    col_total = spread_sum(col_total, ("zh", "y", "zl"), 32)
    col_new = DECAY * col_old + (1.0 - DECAY) * (col_total / D)
    grad = jnp.concatenate(grads, axis=1)
    rows = jnp.stack([row_total, jnp.sum(grad * grad / col_new[None, :], axis=1)])
    rows = rows + lax.ppermute(rows, "c", [(0, 1), (1, 0)])
    rows = rows + sum(
        lax.ppermute(rows, "x", [(i, (i + d) % 4) for i in range(4)]) for d in (1, 2, 3))
    row_new = DECAY * row_old + (1.0 - DECAY) * (rows[0] / FF)
    pair = jnp.concatenate([rows[1] / row_new, row_new])
    pair = spread_sum(pair, ("zh", "y", "zl"), 32)
    row_mean = jnp.sum(pair[128:]) / D
    pair = jnp.sum(pair[:128])[None]
    update_rms = jnp.sqrt(pair[0] * row_mean / (D * FF))
    scale = jnp.sqrt(row_mean) / jnp.maximum(1.0, update_rms / CLIP)
    update = grad * (scale / jnp.sqrt(row_new))[:, None] * (1.0 / jnp.sqrt(col_new))[None, :]
    return (update, row_new, col_new, update_rms)


def solution(mesh):
    mesh = Mesh(mesh.devices.reshape(4, 4, 2, 4, 2), AXES)
    dp, col = ("zh", "y"), ("x", "c")
    in_specs = (P(dp, "zl"), P(dp, col), P(("zl",) + dp), P(col))
    out_specs = (P(("zl",) + dp, col), P(("zl",) + dp), P(col), P())
    return jax.shard_map(
        per_device, mesh=mesh, in_specs=in_specs, out_specs=out_specs, check_vma=False
    )
```

profile of v0, /device:TPU:6, one launch (start us, length us, event | category | flops | bytes accessed | tf_op | source)
XLA Modules:
  0.0 204.9 jit_solution(15062437681906912032)
XLA Ops:
  2.0 2.2 %copy-done = bf16[1024,2048]{1,0:T(8,128)(2,1)S(1)} copy-done((bf16[1024,2048]{1,0:T(8,128)(2,1)S(1)}, bf16[1024,2048]{1,0:T(8,128)(2,1)}, u32[]{:S(2)}) %copy-start) | copy-done | bytes 4194328
  4.2 3.5 %shard_map.75 = f32[1024,256]{1,0:T(8,128)S(1)} custom-call(s32[8]{0:T(128)S(1)} %slice.193.blocks, bf16[1024,2048]{1,0:T(8,128)(2,1)S(1)} %copy-done, bf16[1024,256]{1,0:T(8,128)(2,1)S(1)} %slice.194.cols), custom_call_target="tpu_custom_call" | custom-call | flops 536870912 | bytes 8388608 | tf_op jit(solution)/shard_map/pallas_call | solution.py:67
  12.9 6.4 %shard_map.76 = (f32[1024,512]{1,0:T(8,128)S(1)}, bf16[2048,1024]{1,0:T(8,128)(2,1)S(1)}, bf16[2048,1024]{1,0:T(8,128)(2,1)S(1)}) custom-call(s32[16]{0:T(128)S(1)} %add.226.blocks, bf16[1024,2048]{1,0:T(8,128)(2,1)S(1)} %copy-done.1, bf16[1024,512]{1,0:T(8,128)(2,1)S(1)} %slice.195.cols), custom_call_target="tpu_custom_call" | custom-call | flops 1073741824 | bytes 8388608 | tf_op jit(solution)/shard_map/pallas_call | solution.py:67
  19.9 3.0 %fusion = f32[1024,384]{1,0:T(8,128)} fusion(bf16[2048,1024]{1,0:T(8,128)(2,1)S(1)} %get-tuple-element.56, bf16[1024,2048]{1,0:T(8,128)(2,1)S(1)} %copy-done.6), kind=kOutput, calls=%fused_computation | convolution fusion | flops 805306368 | bytes 4456448 | tf_op jit(solution)/shard_map/dot_general | solution.py:135
  24.4 2.9 %collective-permute-start.1 = (f32[512,256]{1,0:T(8,128)S(1)}, f32[512,256]{1,0:T(8,128)S(1)}, u32[]{:S(2)}, u32[]{:S(2)}) collective-permute-start(f32[512,256]{1,0:T(8,128)S(1)} %slice_add_fusion.4), channel_id=1, source_target_pairs={{0,48},{1,17},{16,32},{17,1},{32,16},{33,49},{48,0},{49,33},{2,50}... | collective-permute-start | bytes 1572872 | tf_op jit(solution)/shard_map/ppermute | solution.py:29
  27.2 3.3 %collective-permute-start.3 = (f32[1024,384]{1,0:T(8,128)}, f32[1024,384]{1,0:T(8,128)}, u32[]{:S(2)}, u32[]{:S(2)}) collective-permute-start(f32[1024,384]{1,0:T(8,128)} %fusion), channel_id=1, source_target_pairs={{0,64},{1,193},{64,0},{65,129},{128,192},{129,65},{192,128},{193,1... | collective-permute-start | bytes 4718600 | tf_op jit(solution)/shard_map/ppermute | solution.py:29
  30.5 2.6 %fusion.6 = f32[1024,512]{1,0:T(8,128)} fusion(bf16[2048,1024]{1,0:T(8,128)(2,1)S(1)} %get-tuple-element.61, bf16[1024,2048]{1,0:T(8,128)(2,1)S(1)} %copy-done.6), kind=kOutput, calls=%fused_computation.6 | convolution fusion | flops 1073741824 | bytes 5242880 | tf_op jit(solution)/shard_map/dot_general | solution.py:135
  33.1 7.4 %collective-permute-done.1 = f32[512,256]{1,0:T(8,128)S(1)} collective-permute-done((f32[512,256]{1,0:T(8,128)S(1)}, f32[512,256]{1,0:T(8,128)S(1)}, u32[]{:S(2)}, u32[]{:S(2)}) %collective-permute-start.1) | collective-permute-done | bytes 524320 | tf_op jit(solution)/shard_map/ppermute | solution.py:29
  42.8 8.3 %collective-permute-done.4 = f32[1024,512]{1,0:T(8,128)} collective-permute-done((f32[1024,512]{1,0:T(8,128)S(1)}, f32[1024,512]{1,0:T(8,128)}, u32[]{:S(2)}, u32[]{:S(2)}) %collective-permute-start.4) | collective-permute-done | bytes 2097184 | tf_op jit(solution)/shard_map/ppermute | solution.py:29
  51.2 2.6 %slice_add_fusion.1 = f32[512,512]{1,0:T(8,128)S(1)} fusion(f32[1024,512]{1,0:T(8,128)} %collective-permute-done.4, bf16[2048,1024]{1,0:T(8,128)(2,1)} %copy-done.2, bf16[1024,2048]{1,0:T(8,128)(2,1)} %param.5), kind=kOutput, calls=%fused_computation.17 | convolution fusion | flops 537133056 | bytes 4194304 | tf_op jit(solution)/shard_map/dot_general | solution.py:135
  53.8 2.7 %collective-permute-start.6 = (f32[512,512]{1,0:T(8,128)S(1)}, f32[512,512]{1,0:T(8,128)S(1)}, u32[]{:S(2)}, u32[]{:S(2)}) collective-permute-start(f32[512,512]{1,0:T(8,128)S(1)} %slice_add_fusion.1), channel_id=1, source_target_pairs={{0,48},{1,17},{16,32},{17,1},{32,16},{33,49},{48,0},{49,33},{2,50}... | collective-permute-start | bytes 3145736 | tf_op jit(solution)/shard_map/ppermute | solution.py:29
  58.8 3.4 %collective-permute-start.2 = (f32[256,256]{1,0:T(8,128)S(1)}, f32[256,256]{1,0:T(8,128)S(1)}, u32[]{:S(2)}, u32[]{:S(2)}) collective-permute-start(f32[256,256]{1,0:T(8,128)S(1)} %slice.252), channel_id=1, source_target_pairs={{0,64},{1,193},{64,0},{65,129},{128,192},{129,65},{192,128},{193,1... | collective-permute-start | bytes 786440 | tf_op jit(solution)/shard_map/ppermute | solution.py:29
  62.2 4.0 %collective-permute-done.3 = f32[1024,384]{1,0:T(8,128)} collective-permute-done((f32[1024,384]{1,0:T(8,128)}, f32[1024,384]{1,0:T(8,128)}, u32[]{:S(2)}, u32[]{:S(2)}) %collective-permute-start.3) | collective-permute-done | bytes 1572896 | tf_op jit(solution)/shard_map/ppermute | solution.py:29
  68.0 8.4 %collective-permute-start.9 = (f32[512,384]{1,0:T(8,128)S(1)}, f32[512,384]{1,0:T(8,128)S(1)}, u32[]{:S(2)}, u32[]{:S(2)}) collective-permute-start(f32[512,384]{1,0:T(8,128)S(1)} %slice_add_fusion.2), channel_id=1, source_target_pairs={{0,192},{1,65},{64,128},{65,1},{128,64},{129,193},{192,0},{193,129... | collective-permute-start | bytes 2359304 | tf_op jit(solution)/shard_map/ppermute | solution.py:29
  76.4 10.4 %collective-permute-start.5 = (f32[128,256]{1,0:T(8,128)S(1)}, f32[128,256]{1,0:T(8,128)S(1)}, u32[]{:S(2)}, u32[]{:S(2)}) collective-permute-start(f32[128,256]{1,0:T(8,128)S(1)} %slice_add_fusion.15), channel_id=1, source_target_pairs={{0,192},{1,65},{64,128},{65,1},{128,64},{129,193},{192,0},{193,129... | collective-permute-start | bytes 393224 | tf_op jit(solution)/shard_map/ppermute | solution.py:29
  91.7 3.4 %collective-permute-start.8 = (f32[256,512]{1,0:T(8,128)S(1)}, f32[256,512]{1,0:T(8,128)S(1)}, u32[]{:S(2)}, u32[]{:S(2)}) collective-permute-start(f32[256,512]{1,0:T(8,128)S(1)} %slice.254), channel_id=1, source_target_pairs={{0,64},{1,193},{64,0},{65,129},{128,192},{129,65},{192,128},{193,1... | collective-permute-start | bytes 1572872 | tf_op jit(solution)/shard_map/ppermute | solution.py:29
  95.0 2.8 %collective-permute-done.5 = f32[128,256]{1,0:T(8,128)S(1)} collective-permute-done((f32[128,256]{1,0:T(8,128)S(1)}, f32[128,256]{1,0:T(8,128)S(1)}, u32[]{:S(2)}, u32[]{:S(2)}) %collective-permute-start.5) | collective-permute-done | bytes 131104 | tf_op jit(solution)/shard_map/ppermute | solution.py:29
  102.0 5.9 %collective-permute-done.8 = f32[256,512]{1,0:T(8,128)S(1)} collective-permute-done((f32[256,512]{1,0:T(8,128)S(1)}, f32[256,512]{1,0:T(8,128)S(1)}, u32[]{:S(2)}, u32[]{:S(2)}) %collective-permute-start.8) | collective-permute-done | bytes 524320 | tf_op jit(solution)/shard_map/ppermute | solution.py:29
  108.0 5.5 %collective-permute-start.10 = (f32[128,512]{1,0:T(8,128)S(1)}, f32[128,512]{1,0:T(8,128)S(1)}, u32[]{:S(2)}, u32[]{:S(2)}) collective-permute-start(f32[128,512]{1,0:T(8,128)S(1)} %slice_add_fusion.8), channel_id=1, source_target_pairs={{0,192},{1,65},{64,128},{65,1},{128,64},{129,193},{192,0},{193,129... | collective-permute-start | bytes 786440 | tf_op jit(solution)/shard_map/ppermute | solution.py:29
  119.6 3.2 %collective-permute-start.17 = (f32[128,384]{1,0:T(8,128)S(1)}, f32[128,384]{1,0:T(8,128)S(1)}, u32[]{:S(2)}, u32[]{:S(2)}) collective-permute-start(f32[128,384]{1,0:T(8,128)S(1)} %slice_add_fusion.11), channel_id=1, source_target_pairs={{0,48},{1,17},{16,32},{17,1},{32,16},{33,49},{48,0},{49,33},{2,50}... | collective-permute-start | bytes 589832 | tf_op jit(solution)/shard_map/ppermute | solution.py:29
  122.8 6.7 %collective-permute-done.12 = f32[1024,128]{1,0:T(8,128)S(1)} collective-permute-done((f32[1024,128]{1,0:T(8,128)S(1)}, f32[1024,128]{1,0:T(8,128)S(1)}, u32[]{:S(2)}, u32[]{:S(2)}) %collective-permute-start.12) | collective-permute-done | bytes 524320 | tf_op jit(solution)/shard_map/ppermute | solution.py:29
  131.4 2.8 %collective-permute-start.16 = (f32[128,512]{1,0:T(8,128)S(1)}, f32[128,512]{1,0:T(8,128)S(1)}, u32[]{:S(2)}, u32[]{:S(2)}) collective-permute-start(f32[128,512]{1,0:T(8,128)S(1)} %slice_add_fusion.6), channel_id=1, source_target_pairs={{0,192},{1,65},{64,128},{65,1},{128,64},{129,193},{192,0},{193,129... | collective-permute-start | bytes 786440 | tf_op jit(solution)/shard_map/ppermute | solution.py:29
  134.8 2.5 %collective-permute-start.21 = (f32[256,256]{1,0:T(8,128)S(1)}, f32[256,256]{1,0:T(8,128)S(1)}, u32[]{:S(2)}, u32[]{:S(2)}) collective-permute-start(f32[256,256]{1,0:T(8,128)S(1)} %slice.262), channel_id=1, source_target_pairs={{0,64},{1,193},{64,0},{65,129},{128,192},{129,65},{192,128},{193,1... | collective-permute-start | bytes 786440 | tf_op jit(solution)/shard_map/ppermute | solution.py:29
  138.1 2.5 %collective-permute-start.20 = (f32[256,128]{1,0:T(8,128)S(1)}, f32[256,128]{1,0:T(8,128)S(1)}, u32[]{:S(2)}, u32[]{:S(2)}) collective-permute-start(f32[256,128]{1,0:T(8,128)S(1)} %slice.263), channel_id=1, source_target_pairs={{0,64},{1,193},{64,0},{65,129},{128,192},{129,65},{192,128},{193,1... | collective-permute-start | bytes 393224 | tf_op jit(solution)/shard_map/ppermute | solution.py:29
  140.6 7.1 %collective-permute-done.21 = f32[256,256]{1,0:T(8,128)S(1)} collective-permute-done((f32[256,256]{1,0:T(8,128)S(1)}, f32[256,256]{1,0:T(8,128)S(1)}, u32[]{:S(2)}, u32[]{:S(2)}) %collective-permute-start.21) | collective-permute-done | bytes 262176 | tf_op jit(solution)/shard_map/ppermute | solution.py:29
  147.7 4.5 %collective-permute-start.22 = (f32[128,256]{1,0:T(8,128)S(1)}, f32[128,256]{1,0:T(8,128)S(1)}, u32[]{:S(2)}, u32[]{:S(2)}) collective-permute-start(f32[128,256]{1,0:T(8,128)S(1)} %slice_add_fusion.13), channel_id=1, source_target_pairs={{0,192},{1,65},{64,128},{65,1},{128,64},{129,193},{192,0},{193,129... | collective-permute-start | bytes 393224 | tf_op jit(solution)/shard_map/ppermute | solution.py:29
  156.1 3.0 %collective-permute-done.23 = f32[128,128]{1,0:T(8,128)S(1)} collective-permute-done((f32[128,128]{1,0:T(8,128)S(1)}, f32[128,128]{1,0:T(8,128)S(1)}, u32[]{:S(2)}, u32[]{:S(2)}) %collective-permute-start.23) | collective-permute-done | bytes 65568 | tf_op jit(solution)/shard_map/ppermute | solution.py:29
  160.1 4.8 %all-to-all-start = ((f32[32,1,2048]{2,1,0:T(1,128)}), f32[32,1,2048]{2,1,0:T(1,128)S(1)}, u32[]{:S(2)}, u32[]{:S(2)}) async-start(f32[32,1,2048]{2,1,0:T(1,128)} %broadcast_in_dim.4), calls=%async_computation | async-start | bytes 524288 | tf_op jit(solution)/shard_map/all_to_all | solution.py:34
  164.9 11.5 %all-to-all-done = f32[32,1,2048]{2,1,0:T(1,128)S(1)} async-done(((f32[32,1,2048]{2,1,0:T(1,128)}), f32[32,1,2048]{2,1,0:T(1,128)S(1)}, u32[]{:S(2)}, u32[]{:S(2)}) %all-to-all-start) | async-done | bytes 262176 | tf_op jit(solution)/shard_map/all_to_all | solution.py:34
  179.1 2.3 %collective-permute-start.25 = (f32[2,128]{1,0:T(2,128)S(1)}, f32[2,128]{1,0:T(2,128)S(1)}, u32[]{:S(2)}, u32[]{:S(2)}) collective-permute-start(f32[2,128]{1,0:T(2,128)S(1)} %fusion.89), channel_id=1, source_target_pairs={{0,2},{2,4},{4,6},{6,0},{1,3},{3,5},{5,7},{7,1},{8,10},{10,12},{12... | collective-permute-start | bytes 3080 | tf_op jit(solution)/shard_map/ppermute | solution.py:207
  183.0 3.5 %collective-permute-done.26 = f32[2,128]{1,0:T(2,128)S(1)} collective-permute-done((f32[2,128]{1,0:T(2,128)S(1)}, f32[2,128]{1,0:T(2,128)S(1)}, u32[]{:S(2)}, u32[]{:S(2)}) %collective-permute-start.26) | collective-permute-done | bytes 1056 | tf_op jit(solution)/shard_map/ppermute | solution.py:207
  186.6 13.9 %all_to_all.12 = f32[32,1,256]{2,1,0:T(1,128)S(1)} all-to-all(f32[32,1,256]{2,1,0:T(1,128)S(1)} %broadcast_in_dim.5), channel_id=1, replica_groups=mesh['zh'=4,'y'=4,'zl'=2,'x'=4,'c'=2] {'zh','y','zl'}, dimensions={0} | all-to-all | bytes 65536 | tf_op jit(solution)/shard_map/all_to_all | solution.py:34
  (122 shorter events, 44.2 us)
Async XLA Ops:
  7.7 15.2 %collective-permute-start = (f32[1024,256]{1,0:T(8,128)S(1)}, f32[1024,256]{1,0:T(8,128)}, u32[]{:S(2)}, u32[]{:S(2)}) collective-permute-start(f32[1024,256]{1,0:T(8,128)S(1)} %shard_map.75), channel_id=1, source_target_pairs={{0,16},{1,49},{16,0},{17,33},{32,48},{33,17},{48,32},{49,1},{2,18}... | collective-permute-start | bytes 3145736 | tf_op jit(solution)/shard_map/ppermute | solution.py:29
  19.3 31.8 %collective-permute-start.4 = (f32[1024,512]{1,0:T(8,128)S(1)}, f32[1024,512]{1,0:T(8,128)}, u32[]{:S(2)}, u32[]{:S(2)}) collective-permute-start(f32[1024,512]{1,0:T(8,128)S(1)} %get-tuple-element.58), channel_id=1, source_target_pairs={{0,16},{1,49},{16,0},{17,33},{32,48},{33,17},{48,32},{49,1},{2,18}... | collective-permute-start | bytes 6291464 | tf_op jit(solution)/shard_map/ppermute | solution.py:29
  24.4 16.2 %collective-permute-start.1 = (f32[512,256]{1,0:T(8,128)S(1)}, f32[512,256]{1,0:T(8,128)S(1)}, u32[]{:S(2)}, u32[]{:S(2)}) collective-permute-start(f32[512,256]{1,0:T(8,128)S(1)} %slice_add_fusion.4), channel_id=1, source_target_pairs={{0,48},{1,17},{16,32},{17,1},{32,16},{33,49},{48,0},{49,33},{2,50}... | collective-permute-start | bytes 1572872 | tf_op jit(solution)/shard_map/ppermute | solution.py:29
  27.2 38.9 %collective-permute-start.3 = (f32[1024,384]{1,0:T(8,128)}, f32[1024,384]{1,0:T(8,128)}, u32[]{:S(2)}, u32[]{:S(2)}) collective-permute-start(f32[1024,384]{1,0:T(8,128)} %fusion), channel_id=1, source_target_pairs={{0,64},{1,193},{64,0},{65,129},{128,192},{129,65},{192,128},{193,1... | collective-permute-start | bytes 4718600 | tf_op jit(solution)/shard_map/ppermute | solution.py:29
  40.5 46.2 %collective-permute-start.7 = (f32[1024,512]{1,0:T(8,128)}, f32[1024,512]{1,0:T(8,128)}, u32[]{:S(2)}, u32[]{:S(2)}) collective-permute-start(f32[1024,512]{1,0:T(8,128)} %fusion.6), channel_id=1, source_target_pairs={{0,16},{1,49},{16,0},{17,33},{32,48},{33,17},{48,32},{49,1},{2,18}... | collective-permute-start | bytes 6291464 | tf_op jit(solution)/shard_map/ppermute | solution.py:29
  53.8 33.0 %collective-permute-start.6 = (f32[512,512]{1,0:T(8,128)S(1)}, f32[512,512]{1,0:T(8,128)S(1)}, u32[]{:S(2)}, u32[]{:S(2)}) collective-permute-start(f32[512,512]{1,0:T(8,128)S(1)} %slice_add_fusion.1), channel_id=1, source_target_pairs={{0,48},{1,17},{16,32},{17,1},{32,16},{33,49},{48,0},{49,33},{2,50}... | collective-permute-start | bytes 3145736 | tf_op jit(solution)/shard_map/ppermute | solution.py:29
  58.8 17.6 %collective-permute-start.2 = (f32[256,256]{1,0:T(8,128)S(1)}, f32[256,256]{1,0:T(8,128)S(1)}, u32[]{:S(2)}, u32[]{:S(2)}) collective-permute-start(f32[256,256]{1,0:T(8,128)S(1)} %slice.252), channel_id=1, source_target_pairs={{0,64},{1,193},{64,0},{65,129},{128,192},{129,65},{192,128},{193,1... | collective-permute-start | bytes 786440 | tf_op jit(solution)/shard_map/ppermute | solution.py:29
  68.0 29.8 %collective-permute-start.9 = (f32[512,384]{1,0:T(8,128)S(1)}, f32[512,384]{1,0:T(8,128)S(1)}, u32[]{:S(2)}, u32[]{:S(2)}) collective-permute-start(f32[512,384]{1,0:T(8,128)S(1)} %slice_add_fusion.2), channel_id=1, source_target_pairs={{0,192},{1,65},{64,128},{65,1},{128,64},{129,193},{192,0},{193,129... | collective-permute-start | bytes 2359304 | tf_op jit(solution)/shard_map/ppermute | solution.py:29
  76.4 21.4 %collective-permute-start.5 = (f32[128,256]{1,0:T(8,128)S(1)}, f32[128,256]{1,0:T(8,128)S(1)}, u32[]{:S(2)}, u32[]{:S(2)}) collective-permute-start(f32[128,256]{1,0:T(8,128)S(1)} %slice_add_fusion.15), channel_id=1, source_target_pairs={{0,192},{1,65},{64,128},{65,1},{128,64},{129,193},{192,0},{193,129... | collective-permute-start | bytes 393224 | tf_op jit(solution)/shard_map/ppermute | solution.py:29
  88.7 24.7 %collective-permute-start.11 = (f32[512,512]{1,0:T(8,128)S(1)}, f32[512,512]{1,0:T(8,128)S(1)}, u32[]{:S(2)}, u32[]{:S(2)}) collective-permute-start(f32[512,512]{1,0:T(8,128)S(1)} %slice_add_fusion), channel_id=1, source_target_pairs={{0,48},{1,17},{16,32},{17,1},{32,16},{33,49},{48,0},{49,33},{2,50}... | collective-permute-start | bytes 3145736 | tf_op jit(solution)/shard_map/ppermute | solution.py:29
  91.7 16.2 %collective-permute-start.8 = (f32[256,512]{1,0:T(8,128)S(1)}, f32[256,512]{1,0:T(8,128)S(1)}, u32[]{:S(2)}, u32[]{:S(2)}) collective-permute-start(f32[256,512]{1,0:T(8,128)S(1)} %slice.254), channel_id=1, source_target_pairs={{0,64},{1,193},{64,0},{65,129},{128,192},{129,65},{192,128},{193,1... | collective-permute-start | bytes 1572872 | tf_op jit(solution)/shard_map/ppermute | solution.py:29
  99.8 19.8 %collective-permute-start.13 = (f32[256,384]{1,0:T(8,128)S(1)}, f32[256,384]{1,0:T(8,128)S(1)}, u32[]{:S(2)}, u32[]{:S(2)}) collective-permute-start(f32[256,384]{1,0:T(8,128)S(1)} %slice.256), channel_id=1, source_target_pairs={{0,16},{1,49},{16,0},{17,33},{32,48},{33,17},{48,32},{49,1},{2,18}... | collective-permute-start | bytes 1179656 | tf_op jit(solution)/shard_map/ppermute | solution.py:29
  99.9 19.0 %collective-permute-start.14 = (f32[1024,256]{1,0:T(8,128)S(1)}, f32[1024,256]{1,0:T(8,128)S(1)}, u32[]{:S(2)}, u32[]{:S(2)}) collective-permute-start(f32[1024,256]{1,0:T(8,128)S(1)} %fusion.4), channel_id=1, source_target_pairs={{0,16},{1,49},{16,0},{17,33},{32,48},{33,17},{48,32},{49,1},{2,18}... | collective-permute-start | bytes 3145736 | tf_op jit(solution)/shard_map/ppermute | solution.py:29
  108.0 22.1 %collective-permute-start.10 = (f32[128,512]{1,0:T(8,128)S(1)}, f32[128,512]{1,0:T(8,128)S(1)}, u32[]{:S(2)}, u32[]{:S(2)}) collective-permute-start(f32[128,512]{1,0:T(8,128)S(1)} %slice_add_fusion.8), channel_id=1, source_target_pairs={{0,192},{1,65},{64,128},{65,1},{128,64},{129,193},{192,0},{193,129... | collective-permute-start | bytes 786440 | tf_op jit(solution)/shard_map/ppermute | solution.py:29
  115.5 15.9 %collective-permute-start.15 = (f32[256,512]{1,0:T(8,128)S(1)}, f32[256,512]{1,0:T(8,128)S(1)}, u32[]{:S(2)}, u32[]{:S(2)}) collective-permute-start(f32[256,512]{1,0:T(8,128)S(1)} %slice.258), channel_id=1, source_target_pairs={{0,64},{1,193},{64,0},{65,129},{128,192},{129,65},{192,128},{193,1... | collective-permute-start | bytes 1572872 | tf_op jit(solution)/shard_map/ppermute | solution.py:29
  117.4 12.0 %collective-permute-start.12 = (f32[1024,128]{1,0:T(8,128)S(1)}, f32[1024,128]{1,0:T(8,128)S(1)}, u32[]{:S(2)}, u32[]{:S(2)}) collective-permute-start(f32[1024,128]{1,0:T(8,128)S(1)} %fusion.2), channel_id=1, source_target_pairs={{0,16},{1,49},{16,0},{17,33},{32,48},{33,17},{48,32},{49,1},{2,18}... | collective-permute-start | bytes 1572872 | tf_op jit(solution)/shard_map/ppermute | solution.py:29
  119.3 15.0 %collective-permute-start.19 = (f32[512,256]{1,0:T(8,128)S(1)}, f32[512,256]{1,0:T(8,128)S(1)}, u32[]{:S(2)}, u32[]{:S(2)}) collective-permute-start(f32[512,256]{1,0:T(8,128)S(1)} %slice_add_fusion.3), channel_id=1, source_target_pairs={{0,48},{1,17},{16,32},{17,1},{32,16},{33,49},{48,0},{49,33},{2,50}... | collective-permute-start | bytes 1572872 | tf_op jit(solution)/shard_map/ppermute | solution.py:29
  119.6 34.3 %collective-permute-start.17 = (f32[128,384]{1,0:T(8,128)S(1)}, f32[128,384]{1,0:T(8,128)S(1)}, u32[]{:S(2)}, u32[]{:S(2)}) collective-permute-start(f32[128,384]{1,0:T(8,128)S(1)} %slice_add_fusion.11), channel_id=1, source_target_pairs={{0,48},{1,17},{16,32},{17,1},{32,16},{33,49},{48,0},{49,33},{2,50}... | collective-permute-start | bytes 589832 | tf_op jit(solution)/shard_map/ppermute | solution.py:29
  130.0 7.7 %collective-permute-start.18 = (f32[512,128]{1,0:T(8,128)S(1)}, f32[512,128]{1,0:T(8,128)S(1)}, u32[]{:S(2)}, u32[]{:S(2)}) collective-permute-start(f32[512,128]{1,0:T(8,128)S(1)} %slice_add_fusion.9), channel_id=1, source_target_pairs={{0,48},{1,17},{16,32},{17,1},{32,16},{33,49},{48,0},{49,33},{2,50}... | collective-permute-start | bytes 786440 | tf_op jit(solution)/shard_map/ppermute | solution.py:29
  131.4 22.6 %collective-permute-start.16 = (f32[128,512]{1,0:T(8,128)S(1)}, f32[128,512]{1,0:T(8,128)S(1)}, u32[]{:S(2)}, u32[]{:S(2)}) collective-permute-start(f32[128,512]{1,0:T(8,128)S(1)} %slice_add_fusion.6), channel_id=1, source_target_pairs={{0,192},{1,65},{64,128},{65,1},{128,64},{129,193},{192,0},{193,129... | collective-permute-start | bytes 786440 | tf_op jit(solution)/shard_map/ppermute | solution.py:29
  134.8 12.9 %collective-permute-start.21 = (f32[256,256]{1,0:T(8,128)S(1)}, f32[256,256]{1,0:T(8,128)S(1)}, u32[]{:S(2)}, u32[]{:S(2)}) collective-permute-start(f32[256,256]{1,0:T(8,128)S(1)} %slice.262), channel_id=1, source_target_pairs={{0,64},{1,193},{64,0},{65,129},{128,192},{129,65},{192,128},{193,1... | collective-permute-start | bytes 786440 | tf_op jit(solution)/shard_map/ppermute | solution.py:29
  137.4 39.3 %copy-start.9 = (f32[2048]{0:T(1024)S(1)}, f32[2048]{0:T(1024)}, u32[]{:S(2)}) copy-start(f32[2048]{0:T(1024)} %param.7) | copy-start | bytes 24580
  137.4 49.1 %copy-start.11 = (f32[128]{0:T(128)S(1)}, f32[128]{0:T(128)}, u32[]{:S(2)}) copy-start(f32[128]{0:T(128)} %param.6) | copy-start | bytes 1540
  138.1 14.1 %collective-permute-start.20 = (f32[256,128]{1,0:T(8,128)S(1)}, f32[256,128]{1,0:T(8,128)S(1)}, u32[]{:S(2)}, u32[]{:S(2)}) collective-permute-start(f32[256,128]{1,0:T(8,128)S(1)} %slice.263), channel_id=1, source_target_pairs={{0,64},{1,193},{64,0},{65,129},{128,192},{129,65},{192,128},{193,1... | collective-permute-start | bytes 393224 | tf_op jit(solution)/shard_map/ppermute | solution.py:29
  147.7 8.2 %collective-permute-start.22 = (f32[128,256]{1,0:T(8,128)S(1)}, f32[128,256]{1,0:T(8,128)S(1)}, u32[]{:S(2)}, u32[]{:S(2)}) collective-permute-start(f32[128,256]{1,0:T(8,128)S(1)} %slice_add_fusion.13), channel_id=1, source_target_pairs={{0,192},{1,65},{64,128},{65,1},{128,64},{129,193},{192,0},{193,129... | collective-permute-start | bytes 393224 | tf_op jit(solution)/shard_map/ppermute | solution.py:29
  152.3 6.8 %collective-permute-start.23 = (f32[128,128]{1,0:T(8,128)S(1)}, f32[128,128]{1,0:T(8,128)S(1)}, u32[]{:S(2)}, u32[]{:S(2)}) collective-permute-start(f32[128,128]{1,0:T(8,128)S(1)} %slice_add_fusion.17), channel_id=1, source_target_pairs={{0,192},{1,65},{64,128},{65,1},{128,64},{129,193},{192,0},{193,129... | collective-permute-start | bytes 196616 | tf_op jit(solution)/shard_map/ppermute | solution.py:29
  160.1 16.4 %all-to-all-start = ((f32[32,1,2048]{2,1,0:T(1,128)}), f32[32,1,2048]{2,1,0:T(1,128)S(1)}, u32[]{:S(2)}, u32[]{:S(2)}) async-start(f32[32,1,2048]{2,1,0:T(1,128)} %broadcast_in_dim.4), calls=%async_computation | async-start | bytes 524288 | tf_op jit(solution)/shard_map/all_to_all | solution.py:34
  176.7 27.1 %copy-start.8 = (f32[2048]{0:T(1024)}, f32[2048]{0:T(1024)S(1)}, u32[]{:S(2)}) copy-start(f32[2048]{0:T(1024)S(1)} %get-tuple-element.123) | copy-start | bytes 24580
  176.9 1.2 collective-permute-start.24
  178.1 4.9 %collective-permute-start.27 = (f32[2,128]{1,0:T(2,128)S(1)}, f32[2,128]{1,0:T(2,128)S(1)}, u32[]{:S(2)}, u32[]{:S(2)}) collective-permute-start(f32[2,128]{1,0:T(2,128)S(1)} %fusion.89), channel_id=1, source_target_pairs={{0,6},{2,0},{4,2},{6,4},{1,7},{3,1},{5,3},{7,5},{8,14},{10,8},{12,... | collective-permute-start | bytes 3080 | tf_op jit(solution)/shard_map/ppermute | solution.py:207
  179.1 3.9 %collective-permute-start.25 = (f32[2,128]{1,0:T(2,128)S(1)}, f32[2,128]{1,0:T(2,128)S(1)}, u32[]{:S(2)}, u32[]{:S(2)}) collective-permute-start(f32[2,128]{1,0:T(2,128)S(1)} %fusion.89), channel_id=1, source_target_pairs={{0,2},{2,4},{4,6},{6,0},{1,3},{3,5},{5,7},{7,1},{8,10},{10,12},{12... | collective-permute-start | bytes 3080 | tf_op jit(solution)/shard_map/ppermute | solution.py:207
  181.4 5.1 %collective-permute-start.26 = (f32[2,128]{1,0:T(2,128)S(1)}, f32[2,128]{1,0:T(2,128)S(1)}, u32[]{:S(2)}, u32[]{:S(2)}) collective-permute-start(f32[2,128]{1,0:T(2,128)S(1)} %fusion.89), channel_id=1, source_target_pairs={{0,4},{2,6},{4,0},{6,2},{1,5},{3,7},{5,1},{7,3},{8,12},{10,14},{12... | collective-permute-start | bytes 3080 | tf_op jit(solution)/shard_map/ppermute | solution.py:207
  (9 other events, 82.4 us)
where the time goes:
time: 206 us; the launch traced here: 205 us
  starting transfers between devices  73.9 us (36%)
  waiting for transfers between devices  66.7 us (32%)
  matrix products  25.5 us (12%)
  blocking collectives  13.9 us (7%)
  Pallas kernels  9.9 us (5%)
  local copies, waits for them, and re-layouts  8.08 us (4%)
  between operations  3.69 us (2%)
  other arithmetic  3.26 us (2%)
    ppermute x24, starting transfers between devices, swap(): return lax.ppermute(value, (axis, 'c'), pairs)  65 us
    ppermute x24, waiting for transfers between devices, swap(): return lax.ppermute(value, (axis, 'c'), pairs)  49.6 us
    dot_general x16, matrix products, part(): jnp.dot(lhs[axis][i], columns(chunk), preferred_element_type=jnp.float32)  25.5 us
    all_to_all x1, blocking collectives, spread_sum(): return jnp.sum(lax.all_to_all(copies, axes, 0, 0), axis=0)  13.9 us
    all_to_all x1, waiting for transfers between devices, spread_sum(): return jnp.sum(lax.all_to_all(copies, axes, 0, 0), axis=0)  11.5 us
    pallas_call x2, Pallas kernels, early_product(): pl.pallas_call(kernel, grid_spec=pltpu.PrefetchScalarGridSpec(num_scalar_...  9.9 us
    all_to_all x1, starting transfers between devices, spread_sum(): return jnp.sum(lax.all_to_all(copies, axes, 0, 0), axis=0)  4.8 us
    unnamed x34, local copies, waits for them, and re-layouts  4.51 us
  transfers between devices with their start and end apart: 29, of which 16 were waited for; matrix products, arithmetic and copies ran while one was open for 14% of the time, Pallas kernels for 3%

commit v1 on v0

--- a/solution.py
+++ b/solution.py
@@ -82,6 +82,36 @@
     )(blocks, rows, cols)
 
 
+def last_kernel(pair, scaled, update, rms):
+    sums = jnp.sum(pair[...], axis=0, keepdims=True)
+    row_mean = jnp.sum(sums[:, 128:], axis=1, keepdims=True) / D
+    total_sq = jnp.sum(sums[:, :128], axis=1, keepdims=True) * row_mean
+    update_rms = jnp.sqrt(total_sq / (D * FF))
+    update[...] = scaled[...] * (jnp.sqrt(row_mean) / jnp.maximum(1.0, update_rms / CLIP))
+    rms[...] = jnp.broadcast_to(update_rms, rms.shape)
+
+
+def last_product(pair, scaled):
+    rows, cols = scaled.shape
+    return pl.pallas_call(
+        last_kernel,
+        grid=(2,),
+        in_specs=[
+            pl.BlockSpec(pair.shape, lambda i: (0, 0)),
+            pl.BlockSpec((rows // 2, cols), lambda i: (i, 0)),
+        ],
+        out_specs=[
+            pl.BlockSpec((rows // 2, cols), lambda i: (i, 0)),
+            pl.BlockSpec((8, 128), lambda i: (0, 0)),
+        ],
+        out_shape=[
+            jax.ShapeDtypeStruct(scaled.shape, jnp.float32),
+            jax.ShapeDtypeStruct((8, 128), jnp.float32),
+        ],
+        compiler_params=pltpu.CompilerParams(vmem_limit_bytes=8 * 2**20),
+    )(pair, scaled)
+
+
 class Order:
     def __init__(self):
         self.last = None
@@ -144,7 +174,8 @@
     first, = early_product(first_kernel, blocks[:8], activations, columns("a"))
     a = product_chain("y", "a", first)
     a.start()
-    first, by_y, by_zh = early_product(second_kernel, blocks, order(activations), columns("b"))
+    first, by_y, by_zh = early_product(
+        second_kernel, order(blocks), activations, columns("b"))
     lhs = {"y": quarters(by_y), "zh": quarters(by_zh)}
     b = product_chain("y", "b", first)
     b.start()
@@ -207,13 +238,11 @@
         lax.ppermute(rows, "x", [(i, (i + d) % 4) for i in range(4)]) for d in (1, 2, 3))
     row_new = DECAY * row_old + (1.0 - DECAY) * (rows[0] / FF)
     pair = jnp.concatenate([rows[1] / row_new, row_new])
-    pair = spread_sum(pair, ("zh", "y", "zl"), 32)
-    row_mean = jnp.sum(pair[128:]) / D
-    pair = jnp.sum(pair[:128])[None]
-    update_rms = jnp.sqrt(pair[0] * row_mean / (D * FF))
-    scale = jnp.sqrt(row_mean) / jnp.maximum(1.0, update_rms / CLIP)
-    update = grad * (scale / jnp.sqrt(row_new))[:, None] * (1.0 / jnp.sqrt(col_new))[None, :]
-    return (update, row_new, col_new, update_rms)
+    pair = jnp.broadcast_to(pair[None], (32, 256))
+    pair = lax.all_to_all(pair, ("zh", "y", "zl"), 0, 0)
+    scaled = grad * lax.rsqrt(row_new)[:, None] * lax.rsqrt(col_new)[None, :]
+    update, update_rms = last_product(pair, scaled)
+    return (update, row_new, col_new, update_rms[0, 0])
 
 
 def solution(mesh):

time: 206 us -> 204 us (level)
  blocking collectives: 13.9 us -> 0 us
  waiting for transfers between devices: 66.7 us -> 76.4 us
  starting transfers between devices: 73.9 us -> 78.1 us
  between operations: 3.69 us -> 1.14 us
    all_to_all x1 -> x0, blocking collectives: 13.9 us -> none  [spread_sum(): return jnp.sum(lax.all_to_all(copies, axes, 0, 0), axis=0)]
    all_to_all x0 -> x1, waiting for transfers between devices: none -> 9.77 us  [per_device(): pair = lax.all_to_all(pair, ('zh', 'y', 'zl'), 0, 0)]
    all_to_all x0 -> x1, starting transfers between devices: none -> 4.21 us  [per_device(): pair = lax.all_to_all(pair, ('zh', 'y', 'zl'), 0, 0)]
    unnamed x34 -> x35, local copies, waits for them, and re-layouts: 4.51 us -> 4.51 us
  transfers between devices with their start and end apart: 29 -> 30, of which waited for: 16 -> 17; matrix products, arithmetic and copies ran while one was open for 14% -> 14% of each run, Pallas kernels for 3% -> 3%
where the time goes in v1:
time: 204 us; the launch traced here: 203 us
  starting transfers between devices  78.1 us (38%)
  waiting for transfers between devices  76.4 us (37%)
  matrix products  25.5 us (12%)
  Pallas kernels  11 us (5%)
  local copies, waits for them, and re-layouts  9.21 us (5%)
    ppermute x24, starting transfers between devices, swap(): return lax.ppermute(value, (axis, 'c'), pairs)  65 us
    ppermute x24, waiting for transfers between devices, swap(): return lax.ppermute(value, (axis, 'c'), pairs)  49.6 us
    dot_general x16, matrix products, part(): jnp.dot(lhs[axis][i], columns(chunk), preferred_element_type=jnp.float32)  25.5 us
    all_to_all x1, waiting for transfers between devices, spread_sum(): return jnp.sum(lax.all_to_all(copies, axes, 0, 0), axis=0)  11.5 us
    pallas_call x2, Pallas kernels, early_product(): pl.pallas_call(kernel, grid_spec=pltpu.PrefetchScalarGridSpec(num_scalar_...  9.9 us
    all_to_all x1, waiting for transfers between devices, per_device(): pair = lax.all_to_all(pair, ('zh', 'y', 'zl'), 0, 0)  9.77 us
    all_to_all x1, starting transfers between devices, spread_sum(): return jnp.sum(lax.all_to_all(copies, axes, 0, 0), axis=0)  4.8 us
    unnamed x35, local copies, waits for them, and re-layouts  4.51 us
  transfers between devices with their start and end apart: 30, of which 17 were waited for; matrix products, arithmetic and copies ran while one was open for 14% of the time, Pallas kernels for 3%

profile of v1, /device:TPU:6, one launch (start us, length us, event | category | flops | bytes accessed | tf_op | source)
XLA Modules:
  0.0 203.0 jit_solution(6323280294496327087)
XLA Ops:
  4.2 3.5 %shard_map.75 = f32[1024,256]{1,0:T(8,128)S(1)} custom-call(s32[8]{0:T(128)S(1)} %slice.190.blocks, bf16[1024,2048]{1,0:T(8,128)(2,1)S(1)} %copy-done, bf16[1024,256]{1,0:T(8,128)(2,1)S(1)} %slice.191.cols), custom_call_target="tpu_custom_call" | custom-call | flops 536870912 | bytes 8388608 | tf_op jit(solution)/shard_map/pallas_call | solution.py:67
  12.9 6.4 %shard_map.76 = (f32[1024,512]{1,0:T(8,128)S(1)}, bf16[2048,1024]{1,0:T(8,128)(2,1)S(1)}, bf16[2048,1024]{1,0:T(8,128)(2,1)S(1)}) custom-call(s32[16]{0:T(128)S(1)} %add.226.blocks, bf16[1024,2048]{1,0:T(8,128)(2,1)S(1)} %copy-done.1, bf16[1024,512]{1,0:T(8,128)(2,1)S(1)} %slice.192.cols), custom_call_target="tpu_custom_call" | custom-call | flops 1073741824 | bytes 8388608 | tf_op jit(solution)/shard_map/pallas_call | solution.py:67
  19.9 3.0 %fusion = f32[1024,384]{1,0:T(8,128)} fusion(bf16[2048,1024]{1,0:T(8,128)(2,1)S(1)} %get-tuple-element.58, bf16[1024,2048]{1,0:T(8,128)(2,1)S(1)} %copy-done.6), kind=kOutput, calls=%fused_computation | convolution fusion | flops 805306368 | bytes 4456448 | tf_op jit(solution)/shard_map/dot_general | solution.py:165
  24.4 2.9 %collective-permute-start.1 = (f32[512,256]{1,0:T(8,128)S(1)}, f32[512,256]{1,0:T(8,128)S(1)}, u32[]{:S(2)}, u32[]{:S(2)}) collective-permute-start(f32[512,256]{1,0:T(8,128)S(1)} %slice_add_fusion.4), channel_id=1, source_target_pairs={{0,48},{1,17},{16,32},{17,1},{32,16},{33,49},{48,0},{49,33},{2,50}... | collective-permute-start | bytes 1572872 | tf_op jit(solution)/shard_map/ppermute | solution.py:29
  27.2 3.3 %collective-permute-start.3 = (f32[1024,384]{1,0:T(8,128)}, f32[1024,384]{1,0:T(8,128)}, u32[]{:S(2)}, u32[]{:S(2)}) collective-permute-start(f32[1024,384]{1,0:T(8,128)} %fusion), channel_id=1, source_target_pairs={{0,64},{1,193},{64,0},{65,129},{128,192},{129,65},{192,128},{193,1... | collective-permute-start | bytes 4718600 | tf_op jit(solution)/shard_map/ppermute | solution.py:29
  30.5 2.6 %fusion.6 = f32[1024,512]{1,0:T(8,128)} fusion(bf16[2048,1024]{1,0:T(8,128)(2,1)S(1)} %get-tuple-element.63, bf16[1024,2048]{1,0:T(8,128)(2,1)S(1)} %copy-done.6), kind=kOutput, calls=%fused_computation.6 | convolution fusion | flops 1073741824 | bytes 5242880 | tf_op jit(solution)/shard_map/dot_general | solution.py:165
  33.1 7.4 %collective-permute-done.1 = f32[512,256]{1,0:T(8,128)S(1)} collective-permute-done((f32[512,256]{1,0:T(8,128)S(1)}, f32[512,256]{1,0:T(8,128)S(1)}, u32[]{:S(2)}, u32[]{:S(2)}) %collective-permute-start.1) | collective-permute-done | bytes 524320 | tf_op jit(solution)/shard_map/ppermute | solution.py:29
  42.8 8.3 %collective-permute-done.4 = f32[1024,512]{1,0:T(8,128)} collective-permute-done((f32[1024,512]{1,0:T(8,128)S(1)}, f32[1024,512]{1,0:T(8,128)}, u32[]{:S(2)}, u32[]{:S(2)}) %collective-permute-start.4) | collective-permute-done | bytes 2097184 | tf_op jit(solution)/shard_map/ppermute | solution.py:29
  51.2 2.6 %slice_add_fusion.1 = f32[512,512]{1,0:T(8,128)S(1)} fusion(f32[1024,512]{1,0:T(8,128)} %collective-permute-done.4, bf16[2048,1024]{1,0:T(8,128)(2,1)} %copy-done.2, bf16[1024,2048]{1,0:T(8,128)(2,1)} %param.5), kind=kOutput, calls=%fused_computation.17 | convolution fusion | flops 537133056 | bytes 4194304 | tf_op jit(solution)/shard_map/dot_general | solution.py:165
  53.8 2.7 %collective-permute-start.6 = (f32[512,512]{1,0:T(8,128)S(1)}, f32[512,512]{1,0:T(8,128)S(1)}, u32[]{:S(2)}, u32[]{:S(2)}) collective-permute-start(f32[512,512]{1,0:T(8,128)S(1)} %slice_add_fusion.1), channel_id=1, source_target_pairs={{0,48},{1,17},{16,32},{17,1},{32,16},{33,49},{48,0},{49,33},{2,50}... | collective-permute-start | bytes 3145736 | tf_op jit(solution)/shard_map/ppermute | solution.py:29
  58.8 3.4 %collective-permute-start.2 = (f32[256,256]{1,0:T(8,128)S(1)}, f32[256,256]{1,0:T(8,128)S(1)}, u32[]{:S(2)}, u32[]{:S(2)}) collective-permute-start(f32[256,256]{1,0:T(8,128)S(1)} %slice.248), channel_id=1, source_target_pairs={{0,64},{1,193},{64,0},{65,129},{128,192},{129,65},{192,128},{193,1... | collective-permute-start | bytes 786440 | tf_op jit(solution)/shard_map/ppermute | solution.py:29
  62.2 4.0 %collective-permute-done.3 = f32[1024,384]{1,0:T(8,128)} collective-permute-done((f32[1024,384]{1,0:T(8,128)}, f32[1024,384]{1,0:T(8,128)}, u32[]{:S(2)}, u32[]{:S(2)}) %collective-permute-start.3) | collective-permute-done | bytes 1572896 | tf_op jit(solution)/shard_map/ppermute | solution.py:29
  68.0 8.4 %collective-permute-start.9 = (f32[512,384]{1,0:T(8,128)S(1)}, f32[512,384]{1,0:T(8,128)S(1)}, u32[]{:S(2)}, u32[]{:S(2)}) collective-permute-start(f32[512,384]{1,0:T(8,128)S(1)} %slice_add_fusion.2), channel_id=1, source_target_pairs={{0,192},{1,65},{64,128},{65,1},{128,64},{129,193},{192,0},{193,129... | collective-permute-start | bytes 2359304 | tf_op jit(solution)/shard_map/ppermute | solution.py:29
  76.4 10.4 %collective-permute-start.5 = (f32[128,256]{1,0:T(8,128)S(1)}, f32[128,256]{1,0:T(8,128)S(1)}, u32[]{:S(2)}, u32[]{:S(2)}) collective-permute-start(f32[128,256]{1,0:T(8,128)S(1)} %slice_add_fusion.15), channel_id=1, source_target_pairs={{0,192},{1,65},{64,128},{65,1},{128,64},{129,193},{192,0},{193,129... | collective-permute-start | bytes 393224 | tf_op jit(solution)/shard_map/ppermute | solution.py:29
  91.7 3.4 %collective-permute-start.8 = (f32[256,512]{1,0:T(8,128)S(1)}, f32[256,512]{1,0:T(8,128)S(1)}, u32[]{:S(2)}, u32[]{:S(2)}) collective-permute-start(f32[256,512]{1,0:T(8,128)S(1)} %slice.250), channel_id=1, source_target_pairs={{0,64},{1,193},{64,0},{65,129},{128,192},{129,65},{192,128},{193,1... | collective-permute-start | bytes 1572872 | tf_op jit(solution)/shard_map/ppermute | solution.py:29
  95.0 2.8 %collective-permute-done.5 = f32[128,256]{1,0:T(8,128)S(1)} collective-permute-done((f32[128,256]{1,0:T(8,128)S(1)}, f32[128,256]{1,0:T(8,128)S(1)}, u32[]{:S(2)}, u32[]{:S(2)}) %collective-permute-start.5) | collective-permute-done | bytes 131104 | tf_op jit(solution)/shard_map/ppermute | solution.py:29
  102.0 5.9 %collective-permute-done.8 = f32[256,512]{1,0:T(8,128)S(1)} collective-permute-done((f32[256,512]{1,0:T(8,128)S(1)}, f32[256,512]{1,0:T(8,128)S(1)}, u32[]{:S(2)}, u32[]{:S(2)}) %collective-permute-start.8) | collective-permute-done | bytes 524320 | tf_op jit(solution)/shard_map/ppermute | solution.py:29
  108.0 5.5 %collective-permute-start.10 = (f32[128,512]{1,0:T(8,128)S(1)}, f32[128,512]{1,0:T(8,128)S(1)}, u32[]{:S(2)}, u32[]{:S(2)}) collective-permute-start(f32[128,512]{1,0:T(8,128)S(1)} %slice_add_fusion.8), channel_id=1, source_target_pairs={{0,192},{1,65},{64,128},{65,1},{128,64},{129,193},{192,0},{193,129... | collective-permute-start | bytes 786440 | tf_op jit(solution)/shard_map/ppermute | solution.py:29
  119.6 3.2 %collective-permute-start.17 = (f32[128,384]{1,0:T(8,128)S(1)}, f32[128,384]{1,0:T(8,128)S(1)}, u32[]{:S(2)}, u32[]{:S(2)}) collective-permute-start(f32[128,384]{1,0:T(8,128)S(1)} %slice_add_fusion.11), channel_id=1, source_target_pairs={{0,48},{1,17},{16,32},{17,1},{32,16},{33,49},{48,0},{49,33},{2,50}... | collective-permute-start | bytes 589832 | tf_op jit(solution)/shard_map/ppermute | solution.py:29
  122.8 6.7 %collective-permute-done.12 = f32[1024,128]{1,0:T(8,128)S(1)} collective-permute-done((f32[1024,128]{1,0:T(8,128)S(1)}, f32[1024,128]{1,0:T(8,128)S(1)}, u32[]{:S(2)}, u32[]{:S(2)}) %collective-permute-start.12) | collective-permute-done | bytes 524320 | tf_op jit(solution)/shard_map/ppermute | solution.py:29
  131.4 2.8 %collective-permute-start.16 = (f32[128,512]{1,0:T(8,128)S(1)}, f32[128,512]{1,0:T(8,128)S(1)}, u32[]{:S(2)}, u32[]{:S(2)}) collective-permute-start(f32[128,512]{1,0:T(8,128)S(1)} %slice_add_fusion.6), channel_id=1, source_target_pairs={{0,192},{1,65},{64,128},{65,1},{128,64},{129,193},{192,0},{193,129... | collective-permute-start | bytes 786440 | tf_op jit(solution)/shard_map/ppermute | solution.py:29
  134.8 2.5 %collective-permute-start.21 = (f32[256,256]{1,0:T(8,128)S(1)}, f32[256,256]{1,0:T(8,128)S(1)}, u32[]{:S(2)}, u32[]{:S(2)}) collective-permute-start(f32[256,256]{1,0:T(8,128)S(1)} %slice.258), channel_id=1, source_target_pairs={{0,64},{1,193},{64,0},{65,129},{128,192},{129,65},{192,128},{193,1... | collective-permute-start | bytes 786440 | tf_op jit(solution)/shard_map/ppermute | solution.py:29
  138.1 2.5 %collective-permute-start.20 = (f32[256,128]{1,0:T(8,128)S(1)}, f32[256,128]{1,0:T(8,128)S(1)}, u32[]{:S(2)}, u32[]{:S(2)}) collective-permute-start(f32[256,128]{1,0:T(8,128)S(1)} %slice.259), channel_id=1, source_target_pairs={{0,64},{1,193},{64,0},{65,129},{128,192},{129,65},{192,128},{193,1... | collective-permute-start | bytes 393224 | tf_op jit(solution)/shard_map/ppermute | solution.py:29
  140.6 7.1 %collective-permute-done.21 = f32[256,256]{1,0:T(8,128)S(1)} collective-permute-done((f32[256,256]{1,0:T(8,128)S(1)}, f32[256,256]{1,0:T(8,128)S(1)}, u32[]{:S(2)}, u32[]{:S(2)}) %collective-permute-start.21) | collective-permute-done | bytes 262176 | tf_op jit(solution)/shard_map/ppermute | solution.py:29
  147.7 4.5 %collective-permute-start.22 = (f32[128,256]{1,0:T(8,128)S(1)}, f32[128,256]{1,0:T(8,128)S(1)}, u32[]{:S(2)}, u32[]{:S(2)}) collective-permute-start(f32[128,256]{1,0:T(8,128)S(1)} %slice_add_fusion.13), channel_id=1, source_target_pairs={{0,192},{1,65},{64,128},{65,1},{128,64},{129,193},{192,0},{193,129... | collective-permute-start | bytes 393224 | tf_op jit(solution)/shard_map/ppermute | solution.py:29
  156.1 3.0 %collective-permute-done.23 = f32[128,128]{1,0:T(8,128)S(1)} collective-permute-done((f32[128,128]{1,0:T(8,128)S(1)}, f32[128,128]{1,0:T(8,128)S(1)}, u32[]{:S(2)}, u32[]{:S(2)}) %collective-permute-start.23) | collective-permute-done | bytes 65568 | tf_op jit(solution)/shard_map/ppermute | solution.py:29
  160.1 4.8 %all-to-all-start = ((f32[32,1,2048]{2,1,0:T(1,128)}), f32[32,1,2048]{2,1,0:T(1,128)S(1)}, u32[]{:S(2)}, u32[]{:S(2)}) async-start(f32[32,1,2048]{2,1,0:T(1,128)} %broadcast_in_dim.4), calls=%async_computation | async-start | bytes 524288 | tf_op jit(solution)/shard_map/all_to_all | solution.py:34
  164.9 11.5 %all-to-all-done = f32[32,1,2048]{2,1,0:T(1,128)S(1)} async-done(((f32[32,1,2048]{2,1,0:T(1,128)}), f32[32,1,2048]{2,1,0:T(1,128)S(1)}, u32[]{:S(2)}, u32[]{:S(2)}) %all-to-all-start) | async-done | bytes 262176 | tf_op jit(solution)/shard_map/all_to_all | solution.py:34
  179.0 2.4 %collective-permute-start.25 = (f32[2,128]{1,0:T(2,128)S(1)}, f32[2,128]{1,0:T(2,128)S(1)}, u32[]{:S(2)}, u32[]{:S(2)}) collective-permute-start(f32[2,128]{1,0:T(2,128)S(1)} %fusion.89), channel_id=1, source_target_pairs={{0,2},{2,4},{4,6},{6,0},{1,3},{3,5},{5,7},{7,1},{8,10},{10,12},{12... | collective-permute-start | bytes 3080 | tf_op jit(solution)/shard_map/ppermute | solution.py:238
  183.0 3.5 %collective-permute-done.26 = f32[2,128]{1,0:T(2,128)S(1)} collective-permute-done((f32[2,128]{1,0:T(2,128)S(1)}, f32[2,128]{1,0:T(2,128)S(1)}, u32[]{:S(2)}, u32[]{:S(2)}) %collective-permute-start.26) | collective-permute-done | bytes 1056 | tf_op jit(solution)/shard_map/ppermute | solution.py:238
  187.2 4.2 %all-to-all-start.1 = ((f32[32,1,256]{2,1,0:T(1,128)}), f32[32,1,256]{2,1,0:T(1,128)S(1)}, u32[]{:S(2)}, u32[]{:S(2)}) async-start(f32[32,1,256]{2,1,0:T(1,128)} %broadcast_in_dim.5), calls=%async_computation.1 | async-start | bytes 65536 | tf_op jit(solution)/shard_map/all_to_all | solution.py:242
  191.6 9.8 %all-to-all-done.1 = f32[32,1,256]{2,1,0:T(1,128)S(1)} async-done(((f32[32,1,256]{2,1,0:T(1,128)}), f32[32,1,256]{2,1,0:T(1,128)S(1)}, u32[]{:S(2)}, u32[]{:S(2)}) %all-to-all-start.1) | async-done | bytes 32800 | tf_op jit(solution)/shard_map/all_to_all | solution.py:242
  (124 shorter events, 47.0 us)
Async XLA Ops:
  7.7 15.2 %collective-permute-start = (f32[1024,256]{1,0:T(8,128)S(1)}, f32[1024,256]{1,0:T(8,128)}, u32[]{:S(2)}, u32[]{:S(2)}) collective-permute-start(f32[1024,256]{1,0:T(8,128)S(1)} %shard_map.75), channel_id=1, source_target_pairs={{0,16},{1,49},{16,0},{17,33},{32,48},{33,17},{48,32},{49,1},{2,18}... | collective-permute-start | bytes 3145736 | tf_op jit(solution)/shard_map/ppermute | solution.py:29
  19.3 31.8 %collective-permute-start.4 = (f32[1024,512]{1,0:T(8,128)S(1)}, f32[1024,512]{1,0:T(8,128)}, u32[]{:S(2)}, u32[]{:S(2)}) collective-permute-start(f32[1024,512]{1,0:T(8,128)S(1)} %get-tuple-element.60), channel_id=1, source_target_pairs={{0,16},{1,49},{16,0},{17,33},{32,48},{33,17},{48,32},{49,1},{2,18}... | collective-permute-start | bytes 6291464 | tf_op jit(solution)/shard_map/ppermute | solution.py:29
  24.4 16.2 %collective-permute-start.1 = (f32[512,256]{1,0:T(8,128)S(1)}, f32[512,256]{1,0:T(8,128)S(1)}, u32[]{:S(2)}, u32[]{:S(2)}) collective-permute-start(f32[512,256]{1,0:T(8,128)S(1)} %slice_add_fusion.4), channel_id=1, source_target_pairs={{0,48},{1,17},{16,32},{17,1},{32,16},{33,49},{48,0},{49,33},{2,50}... | collective-permute-start | bytes 1572872 | tf_op jit(solution)/shard_map/ppermute | solution.py:29
  27.2 38.9 %collective-permute-start.3 = (f32[1024,384]{1,0:T(8,128)}, f32[1024,384]{1,0:T(8,128)}, u32[]{:S(2)}, u32[]{:S(2)}) collective-permute-start(f32[1024,384]{1,0:T(8,128)} %fusion), channel_id=1, source_target_pairs={{0,64},{1,193},{64,0},{65,129},{128,192},{129,65},{192,128},{193,1... | collective-permute-start | bytes 4718600 | tf_op jit(solution)/shard_map/ppermute | solution.py:29
  40.5 46.3 %collective-permute-start.7 = (f32[1024,512]{1,0:T(8,128)}, f32[1024,512]{1,0:T(8,128)}, u32[]{:S(2)}, u32[]{:S(2)}) collective-permute-start(f32[1024,512]{1,0:T(8,128)} %fusion.6), channel_id=1, source_target_pairs={{0,16},{1,49},{16,0},{17,33},{32,48},{33,17},{48,32},{49,1},{2,18}... | collective-permute-start | bytes 6291464 | tf_op jit(solution)/shard_map/ppermute | solution.py:29
  53.8 33.0 %collective-permute-start.6 = (f32[512,512]{1,0:T(8,128)S(1)}, f32[512,512]{1,0:T(8,128)S(1)}, u32[]{:S(2)}, u32[]{:S(2)}) collective-permute-start(f32[512,512]{1,0:T(8,128)S(1)} %slice_add_fusion.1), channel_id=1, source_target_pairs={{0,48},{1,17},{16,32},{17,1},{32,16},{33,49},{48,0},{49,33},{2,50}... | collective-permute-start | bytes 3145736 | tf_op jit(solution)/shard_map/ppermute | solution.py:29
  58.8 17.6 %collective-permute-start.2 = (f32[256,256]{1,0:T(8,128)S(1)}, f32[256,256]{1,0:T(8,128)S(1)}, u32[]{:S(2)}, u32[]{:S(2)}) collective-permute-start(f32[256,256]{1,0:T(8,128)S(1)} %slice.248), channel_id=1, source_target_pairs={{0,64},{1,193},{64,0},{65,129},{128,192},{129,65},{192,128},{193,1... | collective-permute-start | bytes 786440 | tf_op jit(solution)/shard_map/ppermute | solution.py:29
  68.0 29.8 %collective-permute-start.9 = (f32[512,384]{1,0:T(8,128)S(1)}, f32[512,384]{1,0:T(8,128)S(1)}, u32[]{:S(2)}, u32[]{:S(2)}) collective-permute-start(f32[512,384]{1,0:T(8,128)S(1)} %slice_add_fusion.2), channel_id=1, source_target_pairs={{0,192},{1,65},{64,128},{65,1},{128,64},{129,193},{192,0},{193,129... | collective-permute-start | bytes 2359304 | tf_op jit(solution)/shard_map/ppermute | solution.py:29
  76.4 21.4 %collective-permute-start.5 = (f32[128,256]{1,0:T(8,128)S(1)}, f32[128,256]{1,0:T(8,128)S(1)}, u32[]{:S(2)}, u32[]{:S(2)}) collective-permute-start(f32[128,256]{1,0:T(8,128)S(1)} %slice_add_fusion.15), channel_id=1, source_target_pairs={{0,192},{1,65},{64,128},{65,1},{128,64},{129,193},{192,0},{193,129... | collective-permute-start | bytes 393224 | tf_op jit(solution)/shard_map/ppermute | solution.py:29
  88.7 24.7 %collective-permute-start.11 = (f32[512,512]{1,0:T(8,128)S(1)}, f32[512,512]{1,0:T(8,128)S(1)}, u32[]{:S(2)}, u32[]{:S(2)}) collective-permute-start(f32[512,512]{1,0:T(8,128)S(1)} %slice_add_fusion), channel_id=1, source_target_pairs={{0,48},{1,17},{16,32},{17,1},{32,16},{33,49},{48,0},{49,33},{2,50}... | collective-permute-start | bytes 3145736 | tf_op jit(solution)/shard_map/ppermute | solution.py:29
  91.7 16.2 %collective-permute-start.8 = (f32[256,512]{1,0:T(8,128)S(1)}, f32[256,512]{1,0:T(8,128)S(1)}, u32[]{:S(2)}, u32[]{:S(2)}) collective-permute-start(f32[256,512]{1,0:T(8,128)S(1)} %slice.250), channel_id=1, source_target_pairs={{0,64},{1,193},{64,0},{65,129},{128,192},{129,65},{192,128},{193,1... | collective-permute-start | bytes 1572872 | tf_op jit(solution)/shard_map/ppermute | solution.py:29
  99.8 19.8 %collective-permute-start.13 = (f32[256,384]{1,0:T(8,128)S(1)}, f32[256,384]{1,0:T(8,128)S(1)}, u32[]{:S(2)}, u32[]{:S(2)}) collective-permute-start(f32[256,384]{1,0:T(8,128)S(1)} %slice.252), channel_id=1, source_target_pairs={{0,16},{1,49},{16,0},{17,33},{32,48},{33,17},{48,32},{49,1},{2,18}... | collective-permute-start | bytes 1179656 | tf_op jit(solution)/shard_map/ppermute | solution.py:29
  99.9 19.0 %collective-permute-start.14 = (f32[1024,256]{1,0:T(8,128)S(1)}, f32[1024,256]{1,0:T(8,128)S(1)}, u32[]{:S(2)}, u32[]{:S(2)}) collective-permute-start(f32[1024,256]{1,0:T(8,128)S(1)} %fusion.4), channel_id=1, source_target_pairs={{0,16},{1,49},{16,0},{17,33},{32,48},{33,17},{48,32},{49,1},{2,18}... | collective-permute-start | bytes 3145736 | tf_op jit(solution)/shard_map/ppermute | solution.py:29
  108.0 22.1 %collective-permute-start.10 = (f32[128,512]{1,0:T(8,128)S(1)}, f32[128,512]{1,0:T(8,128)S(1)}, u32[]{:S(2)}, u32[]{:S(2)}) collective-permute-start(f32[128,512]{1,0:T(8,128)S(1)} %slice_add_fusion.8), channel_id=1, source_target_pairs={{0,192},{1,65},{64,128},{65,1},{128,64},{129,193},{192,0},{193,129... | collective-permute-start | bytes 786440 | tf_op jit(solution)/shard_map/ppermute | solution.py:29
  115.5 15.9 %collective-permute-start.15 = (f32[256,512]{1,0:T(8,128)S(1)}, f32[256,512]{1,0:T(8,128)S(1)}, u32[]{:S(2)}, u32[]{:S(2)}) collective-permute-start(f32[256,512]{1,0:T(8,128)S(1)} %slice.254), channel_id=1, source_target_pairs={{0,64},{1,193},{64,0},{65,129},{128,192},{129,65},{192,128},{193,1... | collective-permute-start | bytes 1572872 | tf_op jit(solution)/shard_map/ppermute | solution.py:29
  117.4 12.0 %collective-permute-start.12 = (f32[1024,128]{1,0:T(8,128)S(1)}, f32[1024,128]{1,0:T(8,128)S(1)}, u32[]{:S(2)}, u32[]{:S(2)}) collective-permute-start(f32[1024,128]{1,0:T(8,128)S(1)} %fusion.2), channel_id=1, source_target_pairs={{0,16},{1,49},{16,0},{17,33},{32,48},{33,17},{48,32},{49,1},{2,18}... | collective-permute-start | bytes 1572872 | tf_op jit(solution)/shard_map/ppermute | solution.py:29
  119.3 15.0 %collective-permute-start.19 = (f32[512,256]{1,0:T(8,128)S(1)}, f32[512,256]{1,0:T(8,128)S(1)}, u32[]{:S(2)}, u32[]{:S(2)}) collective-permute-start(f32[512,256]{1,0:T(8,128)S(1)} %slice_add_fusion.3), channel_id=1, source_target_pairs={{0,48},{1,17},{16,32},{17,1},{32,16},{33,49},{48,0},{49,33},{2,50}... | collective-permute-start | bytes 1572872 | tf_op jit(solution)/shard_map/ppermute | solution.py:29
  119.6 34.3 %collective-permute-start.17 = (f32[128,384]{1,0:T(8,128)S(1)}, f32[128,384]{1,0:T(8,128)S(1)}, u32[]{:S(2)}, u32[]{:S(2)}) collective-permute-start(f32[128,384]{1,0:T(8,128)S(1)} %slice_add_fusion.11), channel_id=1, source_target_pairs={{0,48},{1,17},{16,32},{17,1},{32,16},{33,49},{48,0},{49,33},{2,50}... | collective-permute-start | bytes 589832 | tf_op jit(solution)/shard_map/ppermute | solution.py:29
  130.0 7.7 %collective-permute-start.18 = (f32[512,128]{1,0:T(8,128)S(1)}, f32[512,128]{1,0:T(8,128)S(1)}, u32[]{:S(2)}, u32[]{:S(2)}) collective-permute-start(f32[512,128]{1,0:T(8,128)S(1)} %slice_add_fusion.9), channel_id=1, source_target_pairs={{0,48},{1,17},{16,32},{17,1},{32,16},{33,49},{48,0},{49,33},{2,50}... | collective-permute-start | bytes 786440 | tf_op jit(solution)/shard_map/ppermute | solution.py:29
  131.4 22.6 %collective-permute-start.16 = (f32[128,512]{1,0:T(8,128)S(1)}, f32[128,512]{1,0:T(8,128)S(1)}, u32[]{:S(2)}, u32[]{:S(2)}) collective-permute-start(f32[128,512]{1,0:T(8,128)S(1)} %slice_add_fusion.6), channel_id=1, source_target_pairs={{0,192},{1,65},{64,128},{65,1},{128,64},{129,193},{192,0},{193,129... | collective-permute-start | bytes 786440 | tf_op jit(solution)/shard_map/ppermute | solution.py:29
  134.8 12.9 %collective-permute-start.21 = (f32[256,256]{1,0:T(8,128)S(1)}, f32[256,256]{1,0:T(8,128)S(1)}, u32[]{:S(2)}, u32[]{:S(2)}) collective-permute-start(f32[256,256]{1,0:T(8,128)S(1)} %slice.258), channel_id=1, source_target_pairs={{0,64},{1,193},{64,0},{65,129},{128,192},{129,65},{192,128},{193,1... | collective-permute-start | bytes 786440 | tf_op jit(solution)/shard_map/ppermute | solution.py:29
  137.4 39.3 %copy-start.9 = (f32[2048]{0:T(1024)S(1)}, f32[2048]{0:T(1024)}, u32[]{:S(2)}) copy-start(f32[2048]{0:T(1024)} %param.7) | copy-start | bytes 24580
  137.4 49.1 %copy-start.11 = (f32[128]{0:T(128)S(1)}, f32[128]{0:T(128)}, u32[]{:S(2)}) copy-start(f32[128]{0:T(128)} %param.6) | copy-start | bytes 1540
  138.1 14.1 %collective-permute-start.20 = (f32[256,128]{1,0:T(8,128)S(1)}, f32[256,128]{1,0:T(8,128)S(1)}, u32[]{:S(2)}, u32[]{:S(2)}) collective-permute-start(f32[256,128]{1,0:T(8,128)S(1)} %slice.259), channel_id=1, source_target_pairs={{0,64},{1,193},{64,0},{65,129},{128,192},{129,65},{192,128},{193,1... | collective-permute-start | bytes 393224 | tf_op jit(solution)/shard_map/ppermute | solution.py:29
  147.7 8.2 %collective-permute-start.22 = (f32[128,256]{1,0:T(8,128)S(1)}, f32[128,256]{1,0:T(8,128)S(1)}, u32[]{:S(2)}, u32[]{:S(2)}) collective-permute-start(f32[128,256]{1,0:T(8,128)S(1)} %slice_add_fusion.13), channel_id=1, source_target_pairs={{0,192},{1,65},{64,128},{65,1},{128,64},{129,193},{192,0},{193,129... | collective-permute-start | bytes 393224 | tf_op jit(solution)/shard_map/ppermute | solution.py:29
  152.3 6.8 %collective-permute-start.23 = (f32[128,128]{1,0:T(8,128)S(1)}, f32[128,128]{1,0:T(8,128)S(1)}, u32[]{:S(2)}, u32[]{:S(2)}) collective-permute-start(f32[128,128]{1,0:T(8,128)S(1)} %slice_add_fusion.17), channel_id=1, source_target_pairs={{0,192},{1,65},{64,128},{65,1},{128,64},{129,193},{192,0},{193,129... | collective-permute-start | bytes 196616 | tf_op jit(solution)/shard_map/ppermute | solution.py:29
  160.1 16.4 %all-to-all-start = ((f32[32,1,2048]{2,1,0:T(1,128)}), f32[32,1,2048]{2,1,0:T(1,128)S(1)}, u32[]{:S(2)}, u32[]{:S(2)}) async-start(f32[32,1,2048]{2,1,0:T(1,128)} %broadcast_in_dim.4), calls=%async_computation | async-start | bytes 524288 | tf_op jit(solution)/shard_map/all_to_all | solution.py:34
  176.9 1.2 collective-permute-start.24
  178.1 4.9 %collective-permute-start.27 = (f32[2,128]{1,0:T(2,128)S(1)}, f32[2,128]{1,0:T(2,128)S(1)}, u32[]{:S(2)}, u32[]{:S(2)}) collective-permute-start(f32[2,128]{1,0:T(2,128)S(1)} %fusion.89), channel_id=1, source_target_pairs={{0,6},{2,0},{4,2},{6,4},{1,7},{3,1},{5,3},{7,5},{8,14},{10,8},{12,... | collective-permute-start | bytes 3080 | tf_op jit(solution)/shard_map/ppermute | solution.py:238
  179.0 3.9 %collective-permute-start.25 = (f32[2,128]{1,0:T(2,128)S(1)}, f32[2,128]{1,0:T(2,128)S(1)}, u32[]{:S(2)}, u32[]{:S(2)}) collective-permute-start(f32[2,128]{1,0:T(2,128)S(1)} %fusion.89), channel_id=1, source_target_pairs={{0,2},{2,4},{4,6},{6,0},{1,3},{3,5},{5,7},{7,1},{8,10},{10,12},{12... | collective-permute-start | bytes 3080 | tf_op jit(solution)/shard_map/ppermute | solution.py:238
  181.4 5.1 %collective-permute-start.26 = (f32[2,128]{1,0:T(2,128)S(1)}, f32[2,128]{1,0:T(2,128)S(1)}, u32[]{:S(2)}, u32[]{:S(2)}) collective-permute-start(f32[2,128]{1,0:T(2,128)S(1)} %fusion.89), channel_id=1, source_target_pairs={{0,4},{2,6},{4,0},{6,2},{1,5},{3,7},{5,1},{7,3},{8,12},{10,14},{12... | collective-permute-start | bytes 3080 | tf_op jit(solution)/shard_map/ppermute | solution.py:238
  187.2 14.1 %all-to-all-start.1 = ((f32[32,1,256]{2,1,0:T(1,128)}), f32[32,1,256]{2,1,0:T(1,128)S(1)}, u32[]{:S(2)}, u32[]{:S(2)}) async-start(f32[32,1,256]{2,1,0:T(1,128)} %broadcast_in_dim.5), calls=%async_computation.1 | async-start | bytes 65536 | tf_op jit(solution)/shard_map/all_to_all | solution.py:242
  (10 other events, 108.0 us)
